TPU v7x, 256 devices: a whole 4x4x8 slice. The times are simulated.
256 devices in a mesh: side: 2 (over core), shard: 128 (over z, y, x).
Axes of the slice: x: 4, y: 4, z: 8, core: 2. Of those that a mesh axis runs over, the one named last changes fastest.
Arguments:
- node_table: bfloat16 [2, 65536, 768], P('side', 'shard'), may hold values from -6 to 6
- owner: int32 [2, 32768, 1], P('side', 'shard'), may hold values from 0 to 127; in each aligned block of 256 rows (0 to 255, 256 to 511, ..., all dimensions but the last counted through in order) at most 4 rows name the same one
- local_row: int32 [2, 32768], P('side', 'shard'), may hold values from 0 to 511
- w_in: bfloat16 [2, 768, 1024], P('side'), may hold values from -0.21875 to 0.21875
- w_mid: bfloat16 [2, 1024, 1024], P('side'), may hold values from -0.1875 to 0.1875
- w_out: bfloat16 [2, 1024, 128], P('side'), may hold values from -0.1875 to 0.1875
Outputs:
- grad_in: float32 [2, 768, 1024], P('side')
- grad_mid: float32 [2, 1024, 1024], P('side')
- grad_out: float32 [2, 1024, 128], P('side')
Inputs may be any that keep to these rules, and one draw needn't show every extreme that they name: In each tower, among the 256 pairs of one device at most 4 name the same owner, and that bound is reached.
All inputs are finite; a program needn't handle non-finite values.
Results may differ from a plain program's by a relative error of at most 0.0095.
Values may be sent and summed in bfloat16 or wider, within the bound.
No kernel may reach another device: no remote copies, remote signals or barrier semaphores. Data moves between devices by JAX's collectives and lax.ppermute only.
A program may use at most 128 MiB of HBM per device.

v0:
```python
import math

import jax
import jax.numpy as jnp
from jax import lax
from jax.sharding import PartitionSpec as P


def swapped(value, axis, distance):
    mask = 2**distance
    pairs = [(source, source ^ mask) for source in range(lax.axis_size(axis))]
    return lax.ppermute(value, axis, pairs)


def silu_slope(argument):
    logistic = jax.nn.sigmoid(argument)
    return logistic * (1.0 + argument * (1.0 - logistic))


def on_device(node_table, owner, local_row, w_in, w_mid, w_out):
    hop_table = node_table[0]
    owners = owner[0, :, 0]
    wanted = local_row[0]
    shards = lax.axis_size("shard")
    tok_rows = owners.shape[0]
    capacity = max(2, (2 * tok_rows + shards - 1) // shards)
    onehot = (owners[:, None] == jnp.arange(shards, dtype=jnp.int32)[None, :]).astype(jnp.int32)
    before = jnp.cumsum(onehot, axis=0) - onehot
    slot_rank = jnp.sum(before * onehot, axis=1)
    position = owners * capacity + slot_rank
    request = (
        jnp.full((shards * capacity,), -1, jnp.int32)
        .at[position]
        .set(wanted)
        .reshape(shards, capacity)
    )
    incoming = lax.all_to_all(request, "shard", split_axis=0, concat_axis=0, tiled=True)
    present = incoming >= 0
    picked = jnp.take(hop_table, jnp.maximum(incoming, 0), axis=0)
    picked = jnp.where(present[:, :, None], picked, jnp.zeros_like(picked))
    arrived = lax.all_to_all(picked, "shard", split_axis=0, concat_axis=0, tiled=True)
    features = jnp.take(arrived.reshape(shards * capacity, arrived.shape[2]), position, axis=0)
    weight_in = w_in[0]
    weight_mid = w_mid[0]
    weight_out = w_out[0]
    pre_one = jnp.dot(features, weight_in, preferred_element_type=jnp.float32)
    hidden_one = jax.nn.silu(pre_one).astype(jnp.bfloat16)
    pre_two = jnp.dot(hidden_one, weight_mid, preferred_element_type=jnp.float32)
    hidden_two = jax.nn.silu(pre_two).astype(jnp.bfloat16)
    pre_three = jnp.dot(hidden_two, weight_out, preferred_element_type=jnp.float32)
    inverse_norm = lax.rsqrt(jnp.sum(pre_three * pre_three, axis=-1, keepdims=True) + 1e-06)
    unit_emb = pre_three * inverse_norm
    embedded = unit_emb.astype(jnp.bfloat16)
    partner = swapped(embedded, "side", 0)
    others = lax.all_gather(partner, "shard", axis=0, tiled=True)
    scores = 40.0 * lax.dot_general(
        embedded, others, (((1,), (1,)), ((), ())), preferred_element_type=jnp.float32
    )
    total_rows = shards * tok_rows
    loss_scale = 0.5 / math.sqrt(total_rows)
    first_row = lax.axis_index("shard") * tok_rows
    own_rows = first_row + jnp.arange(tok_rows, dtype=jnp.int32)
    diagonal_mask = (jnp.arange(total_rows, dtype=jnp.int32)[None, :] == own_rows[:, None]).astype(
        jnp.float32
    )
    row_norm = jnp.log(jnp.sum(jnp.exp(scores), axis=1))
    own_grad = ((jnp.exp(scores - row_norm[:, None]) - diagonal_mask) * loss_scale).astype(
        jnp.bfloat16
    )
    row_pull = 40.0 * jnp.dot(own_grad, others, preferred_element_type=jnp.float32)
    column_sum = lax.psum_scatter(
        40.0
        * lax.dot_general(
            own_grad, embedded, (((0,), (0,)), ((), ())), preferred_element_type=jnp.float32
        ),
        "shard",
        scatter_dimension=0,
        tiled=True,
    )
    grad_embed = row_pull + swapped(column_sum, "side", 0)
    along_unit = jnp.sum(grad_embed * unit_emb, axis=-1, keepdims=True)
    back_three = ((grad_embed - unit_emb * along_unit) * inverse_norm).astype(jnp.bfloat16)
    back_two = (
        lax.dot_general(
            back_three, weight_out, (((1,), (1,)), ((), ())), preferred_element_type=jnp.float32
        )
        * silu_slope(pre_two)
    ).astype(jnp.bfloat16)
    back_one = (
        lax.dot_general(
            back_two, weight_mid, (((1,), (1,)), ((), ())), preferred_element_type=jnp.float32
        )
        * silu_slope(pre_one)
    ).astype(jnp.bfloat16)
    sum_out = lax.dot_general(
        hidden_two, back_three, (((0,), (0,)), ((), ())), preferred_element_type=jnp.float32
    )
    sum_mid = lax.dot_general(
        hidden_one, back_two, (((0,), (0,)), ((), ())), preferred_element_type=jnp.float32
    )
    sum_in = lax.dot_general(
        features, back_one, (((0,), (0,)), ((), ())), preferred_element_type=jnp.float32
    )
    totals = lax.psum((sum_in, sum_mid, sum_out), "shard")
    return (totals[0][None], totals[1][None], totals[2][None])


def solution(mesh):
    in_specs = (
        P("side", "shard", None),
        P("side", "shard", None),
        P("side", "shard"),
        P("side", None, None),
        P("side", None, None),
        P("side", None, None),
    )
    out_specs = (P("side", None, None), P("side", None, None), P("side", None, None))
    return jax.shard_map(
        on_device, mesh=mesh, in_specs=in_specs, out_specs=out_specs, check_vma=False
    )
```

profile of v0, /device:TPU:2, one launch (start us, length us, event | category | flops | bytes accessed | tf_op | source)
XLA Modules:
  0.0 1281.5 jit_solution(15712419136184109068)
XLA Ops:
  7.2 0.9 copy.26
  8.1 0.2 fusion.20
  8.4 0.9 fusion.22
  9.3 0.7 compare_select_fusion
  10.0 1.6 scatter_custom_fusion
  11.5 0.1 all_to_all.9
  11.7 26.6 %all_to_all.14 = s32[128,1,4]{2,1,0:T(1,128)S(1)} all-to-all(s32[128,1,4]{2,1,0:T(1,128)S(1)} %bitcast.75), channel_id=1, replica_groups=mesh['side'=2,'shard'=128] {'shard'}, dimensions={0} | all-to-all | bytes 4096 | tf_op jit(solution)/shard_map/all_to_all | solution.py:37
  38.2 0.1 copy.29
  38.3 0.1 copy.30
  38.4 0.1 copy.32
  38.6 0.1 copy.33
  38.7 0.1 reshape.112
  38.8 3.6 gather_fusion
  42.5 1.1 reshape.111
  43.5 2.4 select_select_fusion
  45.9 7.6 all-to-all-start.1
  53.6 0.0 all-gather.2.cloned.1.call-start
  53.7 23.9 %all-to-all-done.1 = bf16[128,4,768]{2,1,0:T(4,128)(2,1)} async-done(((bf16[128,4,768]{2,1,0:T(4,128)(2,1)}), bf16[128,4,768]{2,1,0:T(4,128)(2,1)}, u32[]{:S(2)}, u32[]{:S(2)}) %all-to-all-start.1) | async-done | bytes 786464 | tf_op jit(solution)/shard_map/all_to_all | solution.py:41
  77.5 1.6 reshape.109
  79.1 1.2 gather_fusion.1
  80.3 2.1 fusion.4
  82.4 1.7 multiply_convert_fusion.1
  84.1 0.8 copy-done.3
  84.9 0.3 multiply_reduce_fusion.1
  85.3 0.1 collective-permute-start
  85.4 1.2 collective-permute-done
  86.7 0.6 copy-done.9
  87.3 0.0 all-gather.2.cloned.1.call-update
  87.3 0.2 reduce-scatter.2.cloned.1.call-start
  87.5 127.0 %all-gather.2.cloned.1.call-done = bf16[32768,128]{0,1:T(8,128)(2,1)} async-done(((bf16[256,128]{0,1:T(8,128)(2,1)}), bf16[32768,128]{0,1:T(8,128)(2,1)}) %all-gather.2.cloned.1.call-update) | async-done | bytes 8388624 | tf_op jit(solution)/shard_map/all_gather | solution.py:55
  214.5 16.9 %exponential_reduce_fusion = (f32[256]{0:T(256)S(1)}, f32[256,32768]{1,0:T(8,128)}) fusion(bf16[256,128]{0,1:T(8,128)(2,1)S(1)} %multiply_convert_fusion.4, bf16[32768,128]{0,1:T(8,128)(2,1)} %all-gather.2.cloned.1.call-done), kind=kOutput, calls=%fused_computation.7 | convolution fusion | flops 2164260608 | bytes 42009600 | tf_op jit(solution)/shard_map/dot_general | solution.py:56
  231.5 15.2 %multiply_convert_fusion = bf16[256,32768]{1,0:T(8,128)(2,1)S(1)} fusion(f32[256,32768]{1,0:T(8,128)} %get-tuple-element.13, s32[256]{0:T(256)S(1)} %iota_add_fusion, f32[256]{0:T(256)S(1)} %log.7), kind=kLoop, calls=%fused_computation.5 | loop fusion | flops 50331648 | bytes 50333696 | tf_op jit(solution)/shard_map/convert_element_type | solution.py:67
  246.7 5.7 copy-done.1
  252.4 9.3 convolution_multiply_fusion.1
  261.7 0.0 reduce-scatter.2.cloned.1.call-update
  261.7 0.0 all-reduce.3.cloned.1.call-start
  261.8 723.3 %reduce-scatter.2.cloned.1.call-done = f32[256,128]{0,1:T(8,128)} async-done(((f32[32768,128]{0,1:T(8,128)}), f32[256,128]{0,1:T(8,128)}) %reduce-scatter.2.cloned.1.call-update) | async-done | bytes 131088 | tf_op jit(solution)/shard_map/reduce_scatter | solution.py:71
  985.0 1.6 collective-permute-done.1
  986.6 13.9 %multiply_reduce_fusion = (f32[256]{0:T(256)S(1)}, f32[256,128]{0,1:T(8,128)S(1)}) fusion(f32[256,128]{0,1:T(8,128)S(1)} %get-tuple-element.11, f32[256]{0:T(256)S(1)} %add_rsqrt_fusion, f32[256,128]{0,1:T(8,128)S(1)} %collective-permute-done.1, bf16[256,32768]{1,0:T(8,128)(2,1)} %copy-done.1, bf16[32768,128]{0,1:T(8,128)(2,1)} %all-gather.2.cloned.1.call-done), kind=kOutput, calls=%fused_computation.39 | convolution fusion | flops 2147647232 | bytes 25561088 | tf_op jit(solution)/shard_map/dot_general | solution.py:70
  1000.5 1.1 convolution_bitcast_fusion.2
  1001.7 1.4 fusion.9
  1003.1 4.2 convolution_bitcast_fusion.1
  1007.3 4.0 convolution_bitcast_fusion
  1011.3 0.0 all-reduce.3.cloned.1.call-update
  1011.3 256.7 %all-reduce.3.cloned.1.call-done = (f32[1,768,1024]{2,1,0:T(8,128)}, f32[1,1024,1024]{2,1,0:T(8,128)}, f32[1,1024,128]{2,1,0:T(8,128)}) async-done(((f32[1,768,1024]{2,1,0:T(8,128)}, f32[1,1024,1024]{2,1,0:T(8,128)}, f32[1,1024,128]{2,1,0:T(8,128)}), (f32[1,768,1024]{2,1,0:T(8,128)}, f32[1,1024,1024]{2,1,0:T(8,128)}, f32[1,1024,128]{2,1,0:T(8,128)})) %all-reduce.3.cloned.1.call-update) | async-done | bytes 7864336 | tf_op jit(solution)/shard_map/psum | solution.py:104
  1268.1 4.1 copy.39
  1272.2 2.0 copy.40
  1274.2 0.8 copy.41
  (38 shorter events, 0.2 us)
Async XLA Ops:
  7.2 75.2 %copy-start = (bf16[1,1024,1024]{2,1,0:T(8,128)(2,1)S(1)}, bf16[1,1024,1024]{2,1,0:T(8,128)(2,1)}, u32[]{:S(2)}) copy-start(bf16[1,1024,1024]{2,1,0:T(8,128)(2,1)} %param.10) | copy-start | bytes 6291460
  7.2 46.5 %copy-start.10 = (s32[1,256,1]{1,2,0:T(1,128)S(1)}, s32[1,256,1]{1,2,0:T(1,128)}, u32[]{:S(2)}) copy-start(s32[1,256,1]{1,2,0:T(1,128)} %param.7) | copy-start | bytes 3076
  45.9 31.6 %all-to-all-start.1 = ((bf16[128,4,768]{2,1,0:T(4,128)(2,1)}), bf16[128,4,768]{2,1,0:T(4,128)(2,1)}, u32[]{:S(2)}, u32[]{:S(2)}) async-start(bf16[128,4,768]{2,1,0:T(4,128)(2,1)} %select_select_fusion), calls=%async_computation.1 | async-start | bytes 1572864 | tf_op jit(solution)/shard_map/all_to_all | solution.py:41
  53.6 161.0 %all-gather.2.cloned.1.call-start = ((), (), s32[]{:S(2)}) async-start(), calls=%async_computation.3 | async-start | bytes 8454144 | tf_op jit(solution)/shard_map/all_gather | solution.py:55
  80.3 4.7 copy-start.8
  82.4 2.9 copy-start.5
  84.1 0.8 copy-start.3
  85.3 146.2 %copy-start.6 = (bf16[256,128]{0,1:T(8,128)(2,1)}, bf16[256,128]{0,1:T(8,128)(2,1)S(1)}, u32[]{:S(2)}) copy-start(bf16[256,128]{0,1:T(8,128)(2,1)S(1)} %multiply_convert_fusion.4) | copy-start | bytes 196612
  85.3 1.3 collective-permute-start
  86.7 0.6 copy-start.9
  87.3 897.7 %reduce-scatter.2.cloned.1.call-start = ((), (), s32[]{:S(2)}) async-start(), calls=%async_computation.4 | async-start | bytes 16908288 | tf_op jit(solution)/shard_map/reduce_scatter | solution.py:71
  246.6 5.7 copy-start.1
  261.7 738.8 %copy-start.4 = (bf16[256,1024]{1,0:T(8,128)(2,1)S(1)}, bf16[256,1024]{1,0:T(8,128)(2,1)}, u32[]{:S(2)}) copy-start(bf16[256,1024]{1,0:T(8,128)(2,1)} %copy-done.3) | copy-start | bytes 1572868
  261.7 1006.3 %all-reduce.3.cloned.1.call-start = ((), (), s32[]{:S(2)}) async-start(), calls=%async_computation.5 | async-start | bytes 15728640 | tf_op jit(solution)/shard_map/psum | solution.py:104
  985.0 16.6 %copy-start.11 = (f32[256,1024]{1,0:T(8,128)S(1)}, f32[256,1024]{1,0:T(8,128)}, u32[]{:S(2)}) copy-start(f32[256,1024]{1,0:T(8,128)} %get-tuple-element.9) | copy-start | bytes 3145732
  985.0 1.6 collective-permute-start.1
  1268.1 4.1 copy-start.2
  1268.1 6.1 copy-start.7
Sparse Core Ops, SparseCore 0:
  87.4 127.0 all-gather.1
  261.8 723.1 reduce-scatter.1
  1011.5 256.5 all-reduce.2
where the time goes:
time: 1280 us
  waiting for transfers between devices  1130 us (88%)
  matrix products  55 us (4%)
  blocking collectives  26.6 us (2%)
  local copies, waits for them, and re-layouts  24.7 us (2%)
  other arithmetic  19.5 us (2%)
  between operations  14 us (1%)
    reduce_scatter x1, waiting for transfers between devices, on_device(): lax.psum_scatter(40.0 * lax.dot_general(own_grad, embedded, (((0,), (0,))...  723 us
    psum x1, waiting for transfers between devices, on_device(): totals = lax.psum((sum_in, sum_mid, sum_out), 'shard')  257 us
    all_gather x1, waiting for transfers between devices, on_device(): others = lax.all_gather(partner, 'shard', axis=0, tiled=True)  127 us
    all_to_all x1, blocking collectives, on_device(): lax.all_to_all(request, 'shard', split_axis=0, concat_axis=0, tiled=True)  26.6 us
  transfers between devices with their start and end apart: 6, of which 6 were waited for; matrix products, arithmetic and copies ran while one was open for 0% of the time, Pallas kernels for 0%

commit v1 on v0

v1 whole, which is shorter than its diff:
```python
import math

import jax
import jax.numpy as jnp
from jax import lax
from jax.experimental import pallas as pl
from jax.experimental.pallas import tpu as pltpu
from jax.sharding import Mesh, PartitionSpec as P

NZ, NY, NX = 8, 4, 4
NYX = NY * NX
N_SHARD = NZ * NYX
CAP = 4
ROWS_DEV = 512
TOK = 256
HALF = TOK // 2
FEAT, HID, EMB = 768, 1024, 128
TOKENS = N_SHARD * TOK
UROWS = NZ * HALF
ICOLS = NYX * HALF
EXP2_SCALE = 40.0 / math.log(2.0)
GRAD_SCALE = 40.0 * 0.5 / math.sqrt(TOKENS)
WROWS = FEAT + HID + EMB
PIECE = WROWS // NYX
BF16 = jnp.bfloat16
F32 = jnp.float32
VMEM = pl.BlockSpec(memory_space=pltpu.VMEM)
SMEM = pl.BlockSpec(memory_space=pltpu.SMEM)


def call(kernel, outs, in_specs, scratch=(), mib=48):
    return pl.pallas_call(
        kernel,
        out_shape=[jax.ShapeDtypeStruct(s, d) for s, d in outs],
        in_specs=in_specs,
        out_specs=[VMEM] * len(outs),
        scratch_shapes=list(scratch),
        compiler_params=pltpu.CompilerParams(vmem_limit_bytes=mib * 2**20),
    )


def dot(a, b, dims):
    return lax.dot_general(a, b, (dims, ((), ())), preferred_element_type=F32)


NN = ((1,), (0,))
NT = ((1,), (1,))
TN = ((0,), (0,))


def iota(shape, dim):
    return lax.broadcasted_iota(jnp.int32, shape, dim)


def request_kernel(owner_ref, wanted_ref, request_ref, position_ref):
    own_col = jnp.broadcast_to(owner_ref[...].astype(F32), (TOK, TOK))
    own_row = own_col.T
    earlier = iota((TOK, TOK), 0) < iota((TOK, TOK), 1)
    same = jnp.where((own_col == own_row) & earlier, 1.0, 0.0)
    rank = jnp.sum(same, axis=0, keepdims=True)
    owners = own_row[0:1, :]
    position_ref[...] = (owners * CAP + rank).astype(jnp.int32)
    wanted = wanted_ref[...].astype(F32) + 1.0
    owner_hit = iota((N_SHARD, TOK), 0).astype(F32) == owners
    lanes = iota((N_SHARD, 128), 1)
    request = jnp.zeros((N_SHARD, 128), F32)
    for k in range(CAP):
        hit = jnp.where(owner_hit & (rank == float(k)), wanted, 0.0)
        slot = jnp.sum(hit, axis=1, keepdims=True)
        request = jnp.where(lanes == k, slot, request)
    request_ref[...] = request.astype(jnp.int32) - 1


def pick_kernel(incoming_ref, table_ref, picked_ref):
    slots = N_SHARD * CAP
    spread = jnp.where(iota((slots, N_SHARD), 0) // CAP == iota((slots, N_SHARD), 1), 1.0, 0.0)
    listed = lax.dot_general(
        spread,
        incoming_ref[...].astype(F32),
        (NN, ((), ())),
        precision=lax.Precision.HIGHEST,
        preferred_element_type=F32,
    )
    mine = iota((slots, 128), 0) % CAP == iota((slots, 128), 1)
    row = jnp.sum(jnp.where(mine, listed, 0.0), axis=1, keepdims=True)
    hit = jnp.where(row == iota((slots, ROWS_DEV), 1).astype(F32), 1.0, 0.0).astype(BF16)
    picked_ref[...] = dot(hit, table_ref[...], NN).astype(BF16)


def silu(v):
    return v * (1.0 / (1.0 + jnp.exp(-v)))


def slope(v):
    q = 1.0 / (1.0 + jnp.exp(-v))
    return q * (1.0 + v * (1.0 - q))


def forward_kernel(
    position_ref, arrived_ref, w_in_ref, w_mid_ref, w_out_ref,
    x_ref, z1_ref, z2_ref, u_ref, r_ref, e_ref,
):
    slots = N_SHARD * CAP
    hit = jnp.where(iota((slots, TOK), 0) == position_ref[...], 1.0, 0.0).astype(BF16)
    x = dot(hit, arrived_ref[...], TN).astype(BF16)
    x_ref[...] = x
    z1 = dot(x, w_in_ref[...], NN)
    z1_ref[...] = z1
    z2 = dot(silu(z1).astype(BF16), w_mid_ref[...], NN)
    z2_ref[...] = z2
    z3 = dot(silu(z2).astype(BF16), w_out_ref[...], NN)
    r = lax.rsqrt(jnp.sum(z3 * z3, axis=1, keepdims=True) + 1e-6)
    u = z3 * r
    u_ref[...] = u
    r_ref[...] = jnp.broadcast_to(r, (TOK, EMB))
    e_ref[...] = u.astype(BF16)


CHUNK = 256


def sums_kernel(own_ref, other_ref, items_ref, row_ref, col_ref):
    items = items_ref[...]
    cols = jnp.zeros((8, ICOLS), F32)
    for part, users_ref in ((0, own_ref), (1, other_ref)):
        for c in range(UROWS // CHUNK):
            scores = dot(users_ref[c * CHUNK:(c + 1) * CHUNK, :], items, NT)
            expo = jnp.exp2(scores * EXP2_SCALE)
            cols = cols + jnp.sum(expo.reshape(CHUNK // 8, 8, ICOLS), axis=0)
            folded = expo[:, 0:128]
            for k in range(1, ICOLS // 128):
                folded = folded + expo[:, k * 128:(k + 1) * 128]
            at = part * UROWS + c * CHUNK
            row_ref[:, at:at + CHUNK] = jnp.sum(folded.T, axis=0, keepdims=True)
    col_ref[...] = jnp.sum(cols, axis=0, keepdims=True)


def grad_kernel(
    place_ref, own_ref, other_ref, items_ref, row_ref, col_ref,
    gown_ref, gother_ref, gitems_ref, grad_ref, turned_ref,
):
    items = items_ref[...]
    col_inv = 1.0 / col_ref[...]
    row_inv = 1.0 / row_ref[...]
    z, yx = place_ref[0], place_ref[1]
    for part, users_ref, out_ref in ((0, own_ref, gown_ref), (1, other_ref, gother_ref)):
        for c in range(UROWS // CHUNK):
            users = users_ref[c * CHUNK:(c + 1) * CHUNK, :]
            scores = dot(users, items, NT)
            at = part * UROWS + c * CHUNK
            inv = jnp.broadcast_to(row_inv[:, at:at + CHUNK], (128, CHUNK)).T[:, 0:1]
            grad_ref[...] = jnp.exp2(scores * EXP2_SCALE) * (inv + col_inv)
            if part == 0:
                @pl.when(z // 2 == c)
                def _():
                    rows = pl.ds(pl.multiple_of((z % 2) * HALF, HALF), HALF)
                    columns = pl.ds(pl.multiple_of(yx * HALF, HALF), HALF)
                    eye = iota((HALF, HALF), 0) == iota((HALF, HALF), 1)
                    grad_ref[rows, columns] = grad_ref[rows, columns] - jnp.where(eye, 2.0, 0.0)
            grad = grad_ref[...].astype(BF16)
            pull = dot(grad, items, NN) * GRAD_SCALE
            out_ref[c * CHUNK:(c + 1) * CHUNK, :] = pull.astype(BF16)
            term = dot(users, grad, TN)
            if part == 0 and c == 0:
                turned_ref[...] = term
            else:
                turned_ref[...] += term
    gitems_ref[...] = (turned_ref[...] * GRAD_SCALE).T.astype(BF16)


def backward_kernel(
    place_ref, mine_ref, sent_ref, x_ref, z1_ref, z2_ref, u_ref, r_ref, w_mid_ref, w_out_ref,
    out_ref, sums_ref,
):
    first = place_ref[2] == 0
    mine, sent = mine_ref[...], sent_ref[...]
    g = jnp.concatenate([jnp.where(first, mine, sent), jnp.where(first, sent, mine)], axis=0)
    u = u_ref[...]
    along = jnp.sum(g * u, axis=1, keepdims=True)
    dz3 = ((g - u * along) * r_ref[...]).astype(BF16)
    z2 = z2_ref[...]
    h2 = silu(z2).astype(BF16)
    sums_ref[FEAT + HID:, :] = dot(dz3, h2, TN)
    dz2 = (dot(dz3, w_out_ref[...], NT) * slope(z2)).astype(BF16)
    z1 = z1_ref[...]
    h1 = silu(z1).astype(BF16)
    sums_ref[FEAT:FEAT + HID, :] = dot(h1, dz2, TN)
    dz1 = (dot(dz2, w_mid_ref[...], NT) * slope(z1)).astype(BF16)
    sums_ref[0:FEAT, :] = dot(x_ref[...], dz1, TN)
    for q in range(NYX):
        rows = sums_ref[q * PIECE:(q + 1) * PIECE, :]
        pieces = [rows[:, k * 128:(k + 1) * 128] for k in range(NZ)]
        out_ref[q] = jnp.concatenate(pieces, axis=0).astype(BF16)


def finish_kernel(parts_ref, grad_in_ref, grad_mid_ref, grad_out_ref, turned_ref):
    places = ((0, FEAT, grad_in_ref), (FEAT, FEAT + HID, grad_mid_ref), (FEAT + HID, WROWS, turned_ref))
    for q in range(NYX):
        rows = parts_ref[q].astype(F32)
        for start, stop, ref in places:
            low, high = max(start, q * PIECE), min(stop, (q + 1) * PIECE)
            if low >= high:
                continue
            for k in range(NZ):
                piece = rows[k * PIECE + low - q * PIECE:k * PIECE + high - q * PIECE, :]
                ref[low - start:high - start, k * 128:(k + 1) * 128] = piece
    grad_out_ref[...] = turned_ref[...].T


YX = ("y", "x")
ALL = ("z", "y", "x")


def exchange(value, axes):
    return lax.all_to_all(value, axes, split_axis=0, concat_axis=0, tiled=True)


def spread(value, axes, n):
    return exchange(jnp.broadcast_to(value[None], (n,) + value.shape), axes)


def swap(value):
    return lax.ppermute(value, "side", [(0, 1), (1, 0)])


def total(parts):
    return jnp.sum(parts.astype(F32), axis=0)


def on_device(node_table, owner, local_row, w_in, w_mid, w_out):
    side = lax.axis_index("side")
    place = jnp.stack([lax.axis_index("z"), lax.axis_index("y") * NX + lax.axis_index("x"), side])
    place = place.astype(jnp.int32)
    table, weight_in, weight_mid, weight_out = node_table[0], w_in[0], w_mid[0], w_out[0]

    request, position = call(
        request_kernel,
        [((N_SHARD, 128), jnp.int32), ((1, TOK), jnp.int32)],
        [VMEM, VMEM],
    )(owner[0], local_row)
    incoming = exchange(request.reshape(N_SHARD, 1, 128), ALL).reshape(N_SHARD, 128)
    (picked,) = call(
        pick_kernel, [((N_SHARD * CAP, FEAT), BF16)], [VMEM, VMEM]
    )(incoming, table)
    arrived = exchange(picked.reshape(N_SHARD, CAP, FEAT), ALL).reshape(N_SHARD * CAP, FEAT)
    x, z1, z2, u, r, e = call(
        forward_kernel,
        [
            ((TOK, FEAT), BF16), ((TOK, HID), F32), ((TOK, HID), F32),
            ((TOK, EMB), F32), ((TOK, EMB), F32), ((TOK, EMB), BF16),
        ],
        [VMEM] * 5,
    )(position, arrived, weight_in, weight_mid, weight_out)

    partner = swap(e)
    mine, theirs = jnp.where(side == 0, e, partner), jnp.where(side == 0, partner, e)
    user_half = lax.dynamic_slice_in_dim(mine, side * HALF, HALF, 0)
    item_half = lax.dynamic_slice_in_dim(theirs, side * HALF, HALF, 0)
    own_users = spread(user_half, "z", NZ).reshape(UROWS, EMB)
    other_users = swap(own_users)
    items = spread(item_half, YX, NYX).reshape(ICOLS, EMB)

    row, col = call(
        sums_kernel, [((1, 2 * UROWS), F32), ((1, ICOLS), F32)], [VMEM] * 3
    )(own_users, other_users, items)
    row = row.reshape(2, 8, 128)
    row = row + swap(row)[::-1]
    row = total(spread(row, "z", NZ)).reshape(1, 2 * UROWS)
    col = total(spread(col.reshape(ICOLS // 128, 128), YX, NYX)).reshape(1, ICOLS)

    grad_own, grad_other, grad_items = call(
        grad_kernel,
        [((UROWS, EMB), BF16), ((UROWS, EMB), BF16), ((ICOLS, EMB), BF16)],
        [SMEM] + [VMEM] * 5,
        [pltpu.VMEM((CHUNK, ICOLS), F32), pltpu.VMEM((EMB, ICOLS), F32)],
    )(place, own_users, other_users, items, row, col)
    grad_users = (grad_own.astype(F32) + swap(grad_other).astype(F32)).astype(BF16)
    grad_users = total(exchange(grad_users.reshape(NZ, HALF, EMB), "z"))
    grad_items = total(exchange(grad_items.reshape(NYX, HALF, EMB), YX))
    kept = jnp.where(side == 0, grad_users, grad_items)
    sent = swap(jnp.where(side == 0, grad_items, grad_users))

    (sums,) = call(
        backward_kernel,
        [((NYX, NZ * PIECE, 128), BF16)],
        [SMEM] + [VMEM] * 9,
        [pltpu.VMEM((WROWS, HID), F32)],
    )(place, kept, sent, x, z1, z2, u, r, weight_mid, weight_out)
    sums = total(exchange(sums, YX)).astype(BF16)
    sums = total(exchange(sums.reshape(NZ, PIECE, 128), "z")).astype(BF16)
    sums = spread(sums, "z", NZ).reshape(NZ * PIECE, 128)
    sums = spread(sums, YX, NYX)
    grads = call(
        finish_kernel,
        [((FEAT, HID), F32), ((HID, HID), F32), ((HID, EMB), F32)],
        [VMEM],
        [pltpu.VMEM((EMB, HID), F32)],
    )(sums)
    return tuple(g[None] for g in grads)


def solution(mesh):
    cube = Mesh(mesh.devices.reshape(2, NZ, NY, NX), ("side", "z", "y", "x"))
    rows = P("side", ALL, None)
    whole = P("side", None, None)
    return jax.shard_map(
        on_device,
        mesh=cube,
        in_specs=(rows, rows, P("side", ALL), whole, whole, whole),
        out_specs=(whole, whole, whole),
        check_vma=False,
    )
```

time: 1280 us -> 324 us (0.25)
  waiting for transfers between devices: 1130 us -> 38.9 us
  blocking collectives: 26.6 us -> 213 us
  matrix products: 55 us -> 0 us
  Pallas kernels: 0 us -> 23.5 us
  between operations: 14 us -> 0.82 us
    reduce_scatter x1 -> x0, waiting for transfers between devices: 723 us -> none  [on_device(): lax.psum_scatter(40.0 * lax.dot_general(own_grad, embedded, (((0,), (0,))...]
    psum x1 -> x0, waiting for transfers between devices: 257 us -> none  [on_device(): totals = lax.psum((sum_in, sum_mid, sum_out), 'shard')]
    all_to_all x1 -> x8, blocking collectives: 26.6 us -> 213 us  [exchange(): return lax.all_to_all(value, axes, split_axis=0, concat_axis=0, tiled=True)]
    all_gather x1 -> x0, waiting for transfers between devices: 127 us -> none  [on_device(): others = lax.all_gather(partner, 'shard', axis=0, tiled=True)]
    dot_general x10 -> x0, matrix products: 55 us -> none  [the longest x1 16.9 us: on_device(): lax.dot_general(embedded, others, (((1,), (1,)), ((), ())), preferred_ele...]
    pallas_call x0 -> x7, Pallas kernels: none -> 23.5 us  [the longest x1 7.53 us: on_device(): call(grad_kernel, [((UROWS, EMB), BF16), ((UROWS, EMB), BF16), ((ICOLS, E...]
    convert_element_type x3 -> x1, other arithmetic: 15.2 us -> 1.8 us  [on_device(): (grad_own.astype(F32) + swap(grad_other).astype(F32)).astype(BF16)]
    all_to_all x1 -> x4, waiting for transfers between devices: 23.9 us -> 35.3 us  [exchange(): return lax.all_to_all(value, axes, split_axis=0, concat_axis=0, tiled=True)]
  transfers between devices with their start and end apart: 6 -> 9, of which waited for: 6 -> 7; matrix products, arithmetic and copies ran while one was open for 0% -> 2% of each run, Pallas kernels for 0% -> 0%
where the time goes in v1:
time: 324 us; the launch traced here: 322 us
  blocking collectives  213 us (66%)
  waiting for transfers between devices  38.9 us (12%)
  Pallas kernels  23.5 us (7%)
  starting transfers between devices  20.3 us (6%)
  local copies, waits for them, and re-layouts  15.6 us (5%)
  other arithmetic  10.6 us (3%)
    all_to_all x8, blocking collectives, exchange(): return lax.all_to_all(value, axes, split_axis=0, concat_axis=0, tiled=True)  213 us
    all_to_all x4, waiting for transfers between devices, exchange(): return lax.all_to_all(value, axes, split_axis=0, concat_axis=0, tiled=True)  35.3 us
    all_to_all x4, starting transfers between devices, exchange(): return lax.all_to_all(value, axes, split_axis=0, concat_axis=0, tiled=True)  19.9 us
    unnamed x34, local copies, waits for them, and re-layouts  9.68 us
    pallas_call x1, Pallas kernels, on_device(): call(grad_kernel, [((UROWS, EMB), BF16), ((UROWS, EMB), BF16), ((ICOLS, E...  7.53 us
    reduce_sum x6, other arithmetic, total(): return jnp.sum(parts.astype(F32), axis=0)  7.29 us
  transfers between devices with their start and end apart: 9, of which 7 were waited for; matrix products, arithmetic and copies ran while one was open for 2% of the time, Pallas kernels for 0%

profile of v1, /device:TPU:2, one launch (start us, length us, event | category | flops | bytes accessed | tf_op | source)
XLA Modules:
  0.0 322.2 jit_solution(12219973512955598625)
XLA Ops:
  0.7 0.9 copy.12.owner_ref
  1.6 0.7 copy-done.16
  2.6 26.6 %all_to_all.60 = s32[128,1,128]{2,1,0:T(1,128)S(1)} all-to-all(s32[128,1,128]{2,1,0:T(1,128)S(1)} %bitcast.38), channel_id=1, replica_groups=mesh['side'=2,'z'=8,'y'=4,'x'=4] {'z','y','x'}, dimensions={0} | all-to-all | bytes 131072 | tf_op jit(solution)/shard_map/all_to_all | solution.py:215
  29.2 1.1 copy-done.7
  30.3 1.2 shard_map.86
  31.5 1.1 reshape.50
  32.6 31.8 %all_to_all.61 = bf16[128,4,768]{2,1,0:T(4,128)(2,1)} all-to-all(bf16[128,4,768]{2,1,0:T(4,128)(2,1)} %reshape.50), channel_id=1, replica_groups=mesh['side'=2,'z'=8,'y'=4,'x'=4] {'z','y','x'}, dimensions={0} | all-to-all | bytes 1572864 | tf_op jit(solution)/shard_map/all_to_all | solution.py:215
  64.4 1.6 reshape.51.arrived_ref
  65.9 3.2 %shard_map.87 = (bf16[256,768]{1,0:T(8,128)(2,1)S(1)}, f32[256,1024]{1,0:T(8,128)S(1)}, f32[256,1024]{1,0:T(8,128)S(1)}, f32[256,128]{1,0:T(8,128)S(1)}, f32[256...) custom-call(s32[1,256]{1,0:T(1,128)S(1)} %get-tuple-element.19.position_ref, bf16[512,768]{1,0:T(8,128)(2,1)S(1)} %reshape.51.arrived_ref, ...), custom_call_target="tpu_custom_call" | custom-call | tf_op jit(solution)/shard_map/pallas_call | solution.py:246
  69.2 1.0 copy-done.2
  70.2 1.0 copy-done.4
  71.1 1.3 collective-permute-done
  72.5 14.9 %all_to_all.62 = bf16[8,128,128]{2,1,0:T(8,128)(2,1)S(1)} all-to-all(bf16[8,128,128]{2,1,0:T(8,128)(2,1)S(1)} %broadcast_in_dim.22), channel_id=1, replica_groups=mesh['side'=2,'z'=8,'y'=4,'x'=4] {'z'}, dimensions={0} | all-to-all | bytes 524288 | tf_op jit(solution)/shard_map/all_to_all | solution.py:215
  87.4 0.9 broadcast_in_dim.23
  88.3 4.9 %all-to-all-start.3 = ((bf16[16,128,128]{2,1,0:T(8,128)(2,1)}), bf16[16,128,128]{2,1,0:T(8,128)(2,1)S(1)}, u32[]{:S(2)}, u32[]{:S(2)}) async-start(bf16[16,128,128]{2,1,0:T(8,128)(2,1)} %broadcast_in_dim.23), calls=%async_computation.3 | async-start | bytes 1048576 | tf_op jit(solution)/shard_map/all_to_all | solution.py:215
  93.2 10.7 %all-to-all-done.3 = bf16[16,128,128]{2,1,0:T(8,128)(2,1)S(1)} async-done(((bf16[16,128,128]{2,1,0:T(8,128)(2,1)}), bf16[16,128,128]{2,1,0:T(8,128)(2,1)S(1)}, u32[]{:S(2)}, u32[]{:S(2)}) %all-to-all-start.3) | async-done | bytes 524320 | tf_op jit(solution)/shard_map/all_to_all | solution.py:215
  103.9 2.6 shard_map.88
  106.8 1.2 collective-permute-done.2
  108.0 11.4 %all_to_all.63 = f32[8,2,8,128]{3,2,1,0:T(8,128)} all-to-all(f32[8,2,8,128]{3,2,1,0:T(8,128)S(1)} %broadcast_in_dim.24), channel_id=1, replica_groups=mesh['side'=2,'z'=8,'y'=4,'x'=4] {'z'}, dimensions={0} | all-to-all | bytes 131072 | tf_op jit(solution)/shard_map/all_to_all | solution.py:215
  119.4 0.7 broadcast_in_dim.51
  120.1 5.3 %all-to-all-start.5 = ((f32[16,16,128]{2,1,0:T(8,128)}), f32[16,16,128]{2,1,0:T(8,128)}, u32[]{:S(2)}, u32[]{:S(2)}) async-start(f32[16,16,128]{2,1,0:T(8,128)} %broadcast_in_dim.51), calls=%async_computation.5 | async-start | bytes 262144 | tf_op jit(solution)/shard_map/all_to_all | solution.py:215
  126.1 0.9 reduce_sum.60
  126.9 5.3 %all-to-all-done.5 = f32[16,16,128]{2,1,0:T(8,128)} async-done(((f32[16,16,128]{2,1,0:T(8,128)}), f32[16,16,128]{2,1,0:T(8,128)}, u32[]{:S(2)}, u32[]{:S(2)}) %all-to-all-start.5) | async-done | bytes 131104 | tf_op jit(solution)/shard_map/all_to_all | solution.py:215
  132.2 0.9 reduce_sum.61
  133.8 7.5 %shard_map.89 = (bf16[1024,128]{1,0:T(8,128)(2,1)S(1)}, bf16[1024,128]{1,0:T(8,128)(2,1)}, bf16[2048,128]{1,0:T(8,128)(2,1)S(1)}) custom-call(s32[3]{0:T(128)S(1)} %copy-done.14, bf16[1024,128]{1,0:T(8,128)(2,1)S(1)} %bitcast.31, bf16[1024,128]{1,0:T(8,128)(2,1)S(1)} %collective-permute-done.1.other_ref, bf16[2048,128]{1,0:T(8,128)(2,1)S(1)} %bitcast.28, ...), custom_call_target="tpu_custom_call" | custom-call | tf_op jit(solution)/shard_map/pallas_call | solution.py:271
  141.4 0.8 copy-done.8
  142.2 0.7 copy-done.11
  142.9 5.6 %all-to-all-start.7 = ((bf16[16,128,128]{2,1,0:T(8,128)(2,1)}), bf16[16,128,128]{2,1,0:T(8,128)(2,1)}, u32[]{:S(2)}, u32[]{:S(2)}) async-start(bf16[16,128,128]{2,1,0:T(8,128)(2,1)} %bitcast.36), calls=%async_computation.7 | async-start | bytes 1048576 | tf_op jit(solution)/shard_map/all_to_all | solution.py:215
  148.4 1.8 add_convert_fusion
  150.2 9.4 %all-to-all-done.7 = bf16[16,128,128]{2,1,0:T(8,128)(2,1)} async-done(((bf16[16,128,128]{2,1,0:T(8,128)(2,1)}), bf16[16,128,128]{2,1,0:T(8,128)(2,1)}, u32[]{:S(2)}, u32[]{:S(2)}) %all-to-all-start.7) | async-done | bytes 524320 | tf_op jit(solution)/shard_map/all_to_all | solution.py:215
  159.6 4.0 %all-to-all-start.6 = ((bf16[8,128,128]{2,1,0:T(8,128)(2,1)}), bf16[8,128,128]{2,1,0:T(8,128)(2,1)}, u32[]{:S(2)}, u32[]{:S(2)}) async-start(bf16[8,128,128]{2,1,0:T(8,128)(2,1)} %bitcast.44), calls=%async_computation.6 | async-start | bytes 524288 | tf_op jit(solution)/shard_map/all_to_all | solution.py:215
  163.6 1.8 convert_reduce_fusion
  165.4 9.8 %all-to-all-done.6 = bf16[8,128,128]{2,1,0:T(8,128)(2,1)} async-done(((bf16[8,128,128]{2,1,0:T(8,128)(2,1)}), bf16[8,128,128]{2,1,0:T(8,128)(2,1)}, u32[]{:S(2)}, u32[]{:S(2)}) %all-to-all-start.6) | async-done | bytes 262176 | tf_op jit(solution)/shard_map/all_to_all | solution.py:215
  175.2 1.0 convert_reduce_fusion.1
  176.2 0.9 broadcast_select_fusion.2
  177.2 1.2 collective-permute-done.4.sent_ref
  178.4 1.2 copy-done.5
  179.7 1.0 copy-done.10
  180.6 0.9 copy-done.13
  181.6 0.7 copy-done.15
  182.2 4.9 %shard_map.90 = bf16[16,960,128]{2,1,0:T(8,128)(2,1)} custom-call(s32[3]{0:T(128)S(1)} %copy-done.15, f32[128,128]{1,0:T(8,128)S(1)} %get-tuple-element.36.mine_ref, f32[128,128]{1,0:T(8,128)S(1)} %collective-permute-done.4.sent_ref, bf16[256,768]{1,0:T(8,128)(2,1)S(1)} %copy-done.10, f32[256,1024]{1,0:T(8,128)S(1)} %copy-done.3, f32[256,1024]{1,0:T(8,128)S(1)} %copy-done.5, ...), custom_call_target="tpu_custom_call" | custom-call | tf_op jit(solution)/shard_map/pallas_call | solution.py:283
  187.1 53.4 %all_to_all.64 = bf16[16,960,128]{2,1,0:T(8,128)(2,1)} all-to-all(bf16[16,960,128]{2,1,0:T(8,128)(2,1)} %shard_map.90), channel_id=1, replica_groups=mesh['side'=2,'z'=8,'y'=4,'x'=4] {'y','x'}, dimensions={0} | all-to-all | bytes 7864320 | tf_op jit(solution)/shard_map/all_to_all | solution.py:215
  240.5 2.7 reduce_sum.64
  243.2 13.4 %all_to_all.65 = bf16[8,120,128]{2,1,0:T(8,128)(2,1)S(1)} all-to-all(bf16[8,120,128]{2,1,0:T(8,128)(2,1)S(1)} %bitcast.45), channel_id=1, replica_groups=mesh['side'=2,'z'=8,'y'=4,'x'=4] {'z'}, dimensions={0} | all-to-all | bytes 491520 | tf_op jit(solution)/shard_map/all_to_all | solution.py:215
  256.7 12.7 %all_to_all.66 = bf16[8,120,128]{2,1,0:T(8,128)(2,1)S(1)} all-to-all(bf16[8,120,128]{2,1,0:T(8,128)(2,1)S(1)} %broadcast_in_dim.52), channel_id=1, replica_groups=mesh['side'=2,'z'=8,'y'=4,'x'=4] {'z'}, dimensions={0} | all-to-all | bytes 491520 | tf_op jit(solution)/shard_map/all_to_all | solution.py:215
  269.4 0.8 broadcast_in_dim.54
  270.2 48.3 %all_to_all.67.parts_ref = bf16[16,960,128]{2,1,0:T(8,128)(2,1)S(1)} all-to-all(bf16[16,960,128]{2,1,0:T(8,128)(2,1)S(1)} %broadcast_in_dim.54), channel_id=1, replica_groups=mesh['side'=2,'z'=8,'y'=4,'x'=4] {'y','x'}, dimensions={0} | all-to-all | bytes 7864320 | tf_op jit(solution)/shard_map/all_to_all | solution.py:215
  318.5 3.7 %shard_map.91 = (f32[768,1024]{1,0:T(8,128)}, f32[1024,1024]{1,0:T(8,128)}, f32[1024,128]{1,0:T(8,128)}) custom-call(bf16[16,960,128]{2,1,0:T(8,128)(2,1)S(1)} %all_to_all.67.parts_ref), custom_call_target="tpu_custom_call" | custom-call | tf_op jit(solution)/shard_map/pallas_call | solution.py:293
  (39 shorter events, 2.2 us)
Async XLA Ops:
  0.6 65.3 %copy-start.6 = (bf16[1,1024,128]{2,1,0:T(8,128)(2,1)S(1)}, bf16[1,1024,128]{2,1,0:T(8,128)(2,1)}, u32[]{:S(2)}) copy-start(bf16[1,1024,128]{2,1,0:T(8,128)(2,1)} %param.11) | copy-start | bytes 786436
  0.6 65.3 %copy-start.1 = (bf16[1,768,1024]{2,1,0:T(8,128)(2,1)S(1)}, bf16[1,768,1024]{2,1,0:T(8,128)(2,1)}, u32[]{:S(2)}) copy-start(bf16[1,768,1024]{2,1,0:T(8,128)(2,1)} %param.9) | copy-start | bytes 4718596
  1.6 0.7 copy-start.16
  29.2 1.1 copy-start.7
  69.2 1.0 copy-start.2
  70.2 1.0 copy-start.4
  71.1 16.2 %copy-start.9 = (bf16[256,768]{1,0:T(8,128)(2,1)}, bf16[256,768]{1,0:T(8,128)(2,1)S(1)}, u32[]{:S(2)}) copy-start(bf16[256,768]{1,0:T(8,128)(2,1)S(1)} %get-tuple-element.27.x_ref) | copy-start | bytes 1179652
  71.1 16.2 %copy-start.12 = (f32[256,128]{1,0:T(8,128)}, f32[256,128]{1,0:T(8,128)S(1)}, u32[]{:S(2)}) copy-start(f32[256,128]{1,0:T(8,128)S(1)} %get-tuple-element.31.r_ref) | copy-start | bytes 393220
  71.1 1.3 collective-permute-start
  88.2 90.2 %copy-start = (bf16[1,1024,1024]{2,1,0:T(8,128)(2,1)S(1)}, bf16[1,1024,1024]{2,1,0:T(8,128)(2,1)}, u32[]{:S(2)}) copy-start(bf16[1,1024,1024]{2,1,0:T(8,128)(2,1)} %param.10) | copy-start | bytes 6291460
  88.3 15.7 %all-to-all-start.3 = ((bf16[16,128,128]{2,1,0:T(8,128)(2,1)}), bf16[16,128,128]{2,1,0:T(8,128)(2,1)S(1)}, u32[]{:S(2)}, u32[]{:S(2)}) async-start(bf16[16,128,128]{2,1,0:T(8,128)(2,1)} %broadcast_in_dim.23), calls=%async_computation.3 | async-start | bytes 1048576 | tf_op jit(solution)/shard_map/all_to_all | solution.py:215
  93.2 10.7 %collective-permute-start.1 = (bf16[1024,128]{1,0:T(8,128)(2,1)S(1)}, bf16[1024,128]{1,0:T(8,128)(2,1)S(1)}, u32[]{:S(2)}, u32[]{:S(2)}) collective-permute-start(bf16[1024,128]{1,0:T(8,128)(2,1)S(1)} %bitcast.29), channel_id=1, source_target_pairs={{0,128},{128,0},{1,129},{129,1},{2,130},{130,2},{3,131},{131,3},{4... | collective-permute-start | bytes 786440 | tf_op jit(solution)/shard_map/ppermute | solution.py:223
  106.5 1.4 collective-permute-start.2
  120.1 12.2 %all-to-all-start.5 = ((f32[16,16,128]{2,1,0:T(8,128)}), f32[16,16,128]{2,1,0:T(8,128)}, u32[]{:S(2)}, u32[]{:S(2)}) async-start(f32[16,16,128]{2,1,0:T(8,128)} %broadcast_in_dim.51), calls=%async_computation.5 | async-start | bytes 262144 | tf_op jit(solution)/shard_map/all_to_all | solution.py:215
  133.2 0.7 copy-start.14
  141.4 0.8 copy-start.8
  142.2 0.7 copy-start.11
  142.8 35.6 %copy-start.3 = (f32[256,1024]{1,0:T(8,128)S(1)}, f32[256,1024]{1,0:T(8,128)}, u32[]{:S(2)}) copy-start(f32[256,1024]{1,0:T(8,128)} %copy-done.2) | copy-start | bytes 3145732
  142.9 5.6 %collective-permute-start.3 = (bf16[1024,128]{1,0:T(8,128)(2,1)}, bf16[1024,128]{1,0:T(8,128)(2,1)}, u32[]{:S(2)}, u32[]{:S(2)}) collective-permute-start(bf16[1024,128]{1,0:T(8,128)(2,1)} %get-tuple-element.25), channel_id=1, source_target_pairs={{0,128},{128,0},{1,129},{129,1},{2,130},{130,2},{3,131},{131,3},{4... | collective-permute-start | bytes 786440 | tf_op jit(solution)/shard_map/ppermute | solution.py:223
  142.9 16.7 %all-to-all-start.7 = ((bf16[16,128,128]{2,1,0:T(8,128)(2,1)}), bf16[16,128,128]{2,1,0:T(8,128)(2,1)}, u32[]{:S(2)}, u32[]{:S(2)}) async-start(bf16[16,128,128]{2,1,0:T(8,128)(2,1)} %bitcast.36), calls=%async_computation.7 | async-start | bytes 1048576 | tf_op jit(solution)/shard_map/all_to_all | solution.py:215
  159.6 15.6 %all-to-all-start.6 = ((bf16[8,128,128]{2,1,0:T(8,128)(2,1)}), bf16[8,128,128]{2,1,0:T(8,128)(2,1)}, u32[]{:S(2)}, u32[]{:S(2)}) async-start(bf16[8,128,128]{2,1,0:T(8,128)(2,1)} %bitcast.44), calls=%async_computation.6 | async-start | bytes 524288 | tf_op jit(solution)/shard_map/all_to_all | solution.py:215
  177.1 1.3 collective-permute-start.4
  178.4 1.2 copy-start.5
  179.7 1.0 copy-start.10
  180.6 0.9 copy-start.13
  181.6 0.7 copy-start.15
